TPU v7x, 32 devices: a whole 2x2x4 slice. The times are simulated.
32 devices in a mesh: parts: 2 (over x), dp: 16 (over z, y, core).
Axes of the slice: x: 2, y: 2, z: 4, core: 2. Of those that a mesh axis runs over, the one named last changes fastest.
Arguments:
- mixer_in: bfloat16 [8192, 8192], P(('parts', 'dp')), parts along dimension 0, may hold values from -6 to 6
- gate_in: bfloat16 [8192, 8192], P(('parts', 'dp')), parts along dimension 0, may hold values from -8 to 8
- conv_weight: bfloat16 [4, 8192], replicated, may hold values from -3 to 3
- conv_bias: bfloat16 [8192], replicated, may hold values from -3 to 3
- x_weight: bfloat16 [8192, 288], P('dp'), may hold values from -0.09375 to 0.09375
- dt_weight: bfloat16 [256, 8192], P(None, 'dp'), may hold values from -0.375 to 0.375
- dt_bias: bfloat16 [8192], P('dp'), may hold values from -7 to -2
- a_log: float32 [16, 8192], P(None, 'dp'), may hold values from -3 to 1.5
- d_skip: float32 [8192], P('dp'), may hold values from -4 to 4
- block_slot: int32 [64], P('parts'), parts along dimension 0, may hold values from 0 to 39, as said below
- block_first: int32 [64], P('parts'), parts along dimension 0, may hold values from 0 to 1, as said below
- block_live: int32 [64], P('parts'), parts along dimension 0, may hold values from 1 to 128, as said below
Outputs:
- gated: bfloat16 [8192, 8192], P(('parts', 'dp')), parts along dimension 0
There are 2 independent parts, one for each index of `parts`. A program takes and returns all parts, laid end to end along the dimension named above; an argument that names none is the same for every part. Nothing has to cross between parts.
Inputs may be any that keep to these rules, and one draw needn't show every extreme that they name: `block_slot`: the values are distinct slots. The blocks of one row are consecutive in the incoming order and fill consecutive slots of one lane in that order; a lane holds whole rows; the last lane has all 10 slots used; slot 0 is used; the first block in the incoming order begins a row. `block_first`: agrees with block_slot: 1 exactly for the first block of each row. `block_live`: only the last block of a row can hold fewer than 128 live tokens.
All inputs are finite; a program needn't handle non-finite values.
Results may differ from a plain program's by a relative error of at most 0.0086.
Values may be sent and summed in bfloat16 or wider, within the bound.
A program may use at most 128 MiB of HBM per device.

v0:
```python
import jax
import jax.numpy as jnp
from jax import lax
from jax.sharding import PartitionSpec as P

BLK = 128


def passed_along(block, axis, distance):
    devices = range(lax.axis_size(axis))
    route = [(i - distance, i) for i in devices if i - distance in devices]
    return lax.ppermute(block, axis, route)


def shortened(value):
    return jax.tree.map(lambda a: a.astype(jnp.bfloat16) if a.dtype == jnp.float32 else a, value)


def scan_step(rate, skip, carry, conv_now, delta_now, maps_now, start_now):
    width = rate.shape[0]
    step = delta_now.astype(jnp.float32)
    signal = conv_now.astype(jnp.float32)
    in_map = maps_now[:, :width].astype(jnp.float32)
    out_map = maps_now[:, width:].astype(jnp.float32)
    carry = (
        jnp.exp(step[:, None, :] * rate[None]) * (carry * (1.0 - start_now)[:, None, None])
        + (step * signal)[:, None, :] * in_map[:, :, None]
    )
    result = jnp.sum(carry * out_map[:, :, None], axis=1) + skip[None] * signal
    return (carry, result.astype(jnp.bfloat16))


def body(
    mixer_in,
    gate_in,
    conv_weight,
    conv_bias,
    x_weight,
    dt_weight,
    dt_bias,
    a_log,
    d_skip,
    block_slot,
    block_first,
    block_live,
):
    ndev = lax.axis_size("dp")
    device = lax.axis_index("dp")
    tok_dev, width = mixer_in.shape
    kernel = conv_weight.shape[0]
    state = a_log.shape[0]
    rank = dt_weight.shape[0]
    per_dev = tok_dev // BLK
    local_first = lax.dynamic_slice_in_dim(block_first, device * per_dev, per_dev)
    local_live = lax.dynamic_slice_in_dim(block_live, device * per_dev, per_dev)
    previous = passed_along(mixer_in[tok_dev - (kernel - 1) :], "dp", 1)
    padded = jnp.concatenate([previous, mixer_in], 0)
    offset = jnp.arange(tok_dev, dtype=jnp.int32) % BLK
    first_tok = jnp.repeat(local_first, BLK)
    acc = jnp.zeros((tok_dev, width), jnp.float32) + conv_bias.astype(jnp.float32)[None]
    for tap in range(kernel):
        back = kernel - 1 - tap
        valid = (first_tok == 0) | (offset >= back)
        term = (
            padded[tap : tap + tok_dev].astype(jnp.float32)
            * conv_weight[tap].astype(jnp.float32)[None]
        )
        acc = acc + jnp.where(valid[:, None], term, 0.0)
    convolved = jax.nn.silu(acc).astype(jnp.bfloat16)
    proj = jnp.dot(
        convolved,
        lax.all_gather(x_weight, "dp", axis=0, tiled=True),
        preferred_element_type=jnp.float32,
    ).astype(jnp.bfloat16)
    conv_chan = lax.all_to_all(convolved, "dp", split_axis=1, concat_axis=0, tiled=True)
    proj_all = lax.all_gather(proj, "dp", axis=0, tiled=True)
    summed = (
        jnp.dot(proj_all[:, :rank], dt_weight, preferred_element_type=jnp.float32)
        + dt_bias.astype(jnp.float32)[None]
    )
    delta_chan = jax.nn.softplus(summed).astype(jnp.bfloat16)
    maps_all = proj_all[:, rank:]
    total_tok = conv_chan.shape[0]
    channels = conv_chan.shape[1]
    blocks = total_tok // BLK
    lanes = ndev // 4
    lane_len = 5 * per_dev
    slots = lanes * lane_len
    positions = lane_len * BLK
    src_of_slot = (
        jnp.full((slots,), blocks, jnp.int32)
        .at[block_slot]
        .set(jnp.arange(blocks, dtype=jnp.int32))
    )

    def to_grid(values):
        cols = values.shape[1]
        pieces = values.reshape(blocks, BLK, cols)
        pieces = jnp.concatenate([pieces, jnp.zeros((1, BLK, cols), values.dtype)], 0)
        grid = pieces[src_of_slot].reshape(lanes, positions, cols)
        return jnp.swapaxes(grid, 0, 1)

    first_slot = jnp.concatenate([block_first, jnp.zeros((1,), jnp.int32)], 0)[src_of_slot]
    at_front = (jnp.arange(BLK, dtype=jnp.int32) == 0).astype(jnp.int32)
    start = (first_slot[:, None] * at_front[None]).reshape(lanes, positions).astype(jnp.float32)
    start = jnp.swapaxes(start, 0, 1)
    turns = 20
    stride = positions // turns
    conv_grid = to_grid(conv_chan).reshape(turns, stride, lanes, channels)
    delta_grid = to_grid(delta_chan).reshape(turns, stride, lanes, channels)
    maps_grid = to_grid(maps_all).reshape(turns, stride, lanes, 2 * state)
    start_grid = start.reshape(turns, stride, lanes)
    rate = -jnp.exp(a_log)

    def advance(carry, inputs):
        conv_piece, delta_piece, maps_piece, start_piece = inputs
        results = []
        for inner in range(stride):
            carry, result = scan_step(
                rate,
                d_skip,
                carry,
                conv_piece[inner],
                delta_piece[inner],
                maps_piece[inner],
                start_piece[inner],
            )
            results.append(result)
        return (carry, jnp.stack(results, 0))

    initial = jnp.zeros((lanes, state, channels), jnp.float32)
    carry, outputs = lax.scan(advance, initial, (conv_grid, delta_grid, maps_grid, start_grid))
    outputs = jnp.swapaxes(outputs.reshape(positions, lanes, channels), 0, 1).reshape(
        slots, BLK, channels
    )
    scanned_chan = outputs[block_slot].reshape(total_tok, channels)
    scanned = lax.all_to_all(
        shortened(scanned_chan), "dp", split_axis=0, concat_axis=1, tiled=True
    ).astype(scanned_chan.dtype)
    live = offset < jnp.repeat(local_live, BLK)
    gated = scanned.astype(jnp.float32) * jax.nn.silu(gate_in.astype(jnp.float32))
    return jnp.where(live[:, None], gated, 0.0).astype(jnp.bfloat16)


def solution(mesh):
    in_specs = (
        P(("parts", "dp"), None),
        P(("parts", "dp"), None),
        P(),
        P(),
        P("dp", None),
        P(None, "dp"),
        P("dp"),
        P(None, "dp"),
        P("dp"),
        P("parts"),
        P("parts"),
        P("parts"),
    )
    out_specs = P(("parts", "dp"), None)
    return jax.shard_map(body, mesh=mesh, in_specs=in_specs, out_specs=out_specs, check_vma=False)
```

profile of v0, /device:TPU:13, one launch (start us, length us, event | category | flops | bytes accessed | tf_op | source)
XLA Modules:
  0.0 953.5 jit_solution(6162657398524266983)
XLA Ops:
  8.2 3.7 collective-permute-start
  13.8 6.4 copy.51
  21.3 17.6 %multiply_convert_fusion = bf16[256,8192]{0,1:T(8,128)(2,1)} fusion(bf16[256,8192]{0,1:T(8,128)(2,1)} %copy.51, bf16[3,8192]{0,1:T(8,128)(2,1)S(1)} %copy.50, f32[8192]{0:T(1024)S(1)} %bitcast.2242, f32[8192]{0:T(1024)S(1)} %bitcast.2243, f32[8192]{0:T(1024)S(1)} %bitcast.2241, f32[8192]{0:T(1024)S(1)} %bitcast.2240, f32[8192]{0:T(1024)S(1)} %convert_element_type.3324, ...), kind=kLoop, calls=%fused_computation.1299 | loop fusion | flops 62914560 | bytes 8602624 | tf_op jit(solution)/shard_map/convert_element_type | solution.py:69
  38.9 5.1 all-to-all-start
  44.0 47.4 %all-gather.3.cloned.1.call-done = bf16[8192,288]{0,1:T(8,128)(2,1)} async-done(((bf16[512,288]{0,1:T(8,128)(2,1)}), bf16[8192,288]{0,1:T(8,128)(2,1)}) %all-gather.3.cloned.1.call-update) | async-done | bytes 4718608 | tf_op jit(solution)/shard_map/all_gather | solution.py:72
  91.4 5.7 convolution_convert_fusion
  100.0 65.0 %all-to-all-done = bf16[256,16,512]{0,2,1:T(8,128)(2,1)} async-done(((bf16[256,16,512]{0,2,1:T(8,128)(2,1)}), bf16[256,16,512]{0,2,1:T(8,128)(2,1)}, u32[]{:S(2)}, u32[]{:S(2)}) %all-to-all-start) | async-done | bytes 4194336 | tf_op jit(solution)/shard_map/all_to_all | solution.py:75
  164.9 6.4 copy.55
  171.3 4.8 concatenate.18
  176.1 6.8 gather_fusion.2
  182.9 6.9 fusion.583
  189.8 2.5 concatenate.16
  192.4 6.7 gather_fusion
  199.1 9.1 copy.53
  211.7 602.4 %while.13 = (s32[]{:T(128)}, f32[4,16,512]{2,1,0:T(8,128)S(1)}, bf16[20,64,4,512]{3,1,0,2:T(8,128)(2,1)}, bf16[20,64,4,512]{3,2,1,0:T(4,128)(2,1)}, f32[16,512]{...) while((s32[]{:T(128)}, f32[4,16,512]{2,1,0:T(8,128)S(1)}, ...), condition=%wide.region_66.67_spmd.clone, body=%wide.region_1.66_spmd.clone.sunk | while | flops 21078336 | bytes 15412160 | solution.py:132
  232.5 3.9 multiply_reduce_fusion.83
  245.1 1.8 constant_dynamic-slice_fusion.262
  262.6 3.9 multiply_reduce_fusion.83
  273.7 1.7 constant_dynamic-slice_fusion.263
  292.8 3.9 multiply_reduce_fusion.83
  323.1 3.9 multiply_reduce_fusion.83
  353.1 3.9 multiply_reduce_fusion.83
  362.6 1.7 constant_dynamic-slice_fusion.260
  383.4 3.9 multiply_reduce_fusion.83
  413.5 3.9 multiply_reduce_fusion.83
  443.4 3.9 multiply_reduce_fusion.83
  473.5 3.9 multiply_reduce_fusion.83
  503.4 3.9 multiply_reduce_fusion.83
  533.5 3.9 multiply_reduce_fusion.83
  563.6 3.9 multiply_reduce_fusion.83
  593.5 3.9 multiply_reduce_fusion.83
  606.1 1.8 constant_dynamic-slice_fusion.262
  623.6 3.9 multiply_reduce_fusion.83
  653.7 3.9 multiply_reduce_fusion.83
  683.8 3.9 multiply_reduce_fusion.83
  696.5 1.9 constant_dynamic-slice_fusion.262
  714.1 3.9 multiply_reduce_fusion.83
  744.1 3.9 multiply_reduce_fusion.83
  774.4 3.9 multiply_reduce_fusion.83
  804.6 3.9 multiply_reduce_fusion.83
  814.1 5.3 gather_fusion.4
  819.4 5.2 all-to-all-start.1
  824.7 6.4 copy.63
  831.2 85.9 %all-to-all-done.1 = bf16[16,256,512]{2,1,0:T(8,128)(2,1)} async-done(((bf16[16,256,512]{2,1,0:T(8,128)(2,1)}), bf16[16,256,512]{2,1,0:T(8,128)(2,1)}, u32[]{:S(2)}, u32[]{:S(2)}) %all-to-all-start.1) | async-done | bytes 4194336 | tf_op jit(solution)/shard_map/all_to_all | solution.py:137
  917.1 6.6 convert_bitcast_fusion.128
  923.7 9.3 copy.62
  933.0 7.4 fusion.584
  940.4 6.3 copy.64
  (2810 shorter events, 518.2 us)
Async XLA Ops:
  6.5 176.4 %copy-start = (bf16[256,512]{1,0:T(8,128)(2,1)S(1)}, bf16[256,512]{1,0:T(8,128)(2,1)}, u32[]{:S(2)}) copy-start(bf16[256,512]{1,0:T(8,128)(2,1)} %param.19) | copy-start | bytes 786436
  6.5 13.7 %copy-start.4 = (bf16[8192]{0:T(1024)(128)(2,1)S(1)}, bf16[8192]{0:T(1024)(128)(2,1)}, u32[]{:S(2)}) copy-start(bf16[8192]{0:T(1024)(128)(2,1)} %param.17) | copy-start | bytes 49156
  6.5 84.9 %all-gather.3.cloned.1.call-start = ((), (), s32[]{:S(2)}) async-start(), calls=%async_computation.2 | async-start | bytes 5013504 | tf_op jit(solution)/shard_map/all_gather | solution.py:72
  8.2 12.0 %collective-permute-start = (bf16[3,8192]{1,0:T(4,128)(2,1)S(1)}, bf16[3,8192]{1,0:T(4,128)(2,1)S(1)}, u32[]{:S(2)}, u32[]{:S(2)}) collective-permute-start(bf16[3,8192]{1,0:T(4,128)(2,1)S(1)} %slice.1438), channel_id=1, source_target_pairs={{0,1},{1,2},{2,3},{3,4},{4,5},{5,6},{6,7},{7,8},{8,9},{9,10},{10,1... | collective-permute-start | bytes 147464 | tf_op jit(solution)/shard_map/ppermute | solution.py:12
  38.9 126.0 %all-to-all-start = ((bf16[256,16,512]{0,2,1:T(8,128)(2,1)}), bf16[256,16,512]{0,2,1:T(8,128)(2,1)}, u32[]{:S(2)}, u32[]{:S(2)}) async-start(bf16[256,16,512]{0,2,1:T(8,128)(2,1)} %bitcast.2229), calls=%async_computation | async-start | bytes 8388608 | tf_op jit(solution)/shard_map/all_to_all | solution.py:75
  43.9 53.2 %copy-start.5 = (bf16[512]{0:T(512)(128)(2,1)S(1)}, bf16[512]{0:T(512)(128)(2,1)}, u32[]{:S(2)}) copy-start(bf16[512]{0:T(512)(128)(2,1)} %param.20) | copy-start | bytes 3076
  43.9 53.2 %copy-start.6 = (s32[32]{0:T(128)S(1)}, s32[32]{0:T(128)}, u32[]{:S(2)}) copy-start(s32[32]{0:T(128)} %param.23) | copy-start | bytes 388
  44.0 54.1 %copy-start.7 = (s32[32]{0:T(128)S(1)}, s32[32]{0:T(128)}, u32[]{:S(2)}) copy-start(s32[32]{0:T(128)} %param.24) | copy-start | bytes 388
  44.0 56.0 %copy-start.3 = (f32[16,512]{1,0:T(8,128)S(1)}, f32[16,512]{1,0:T(8,128)}, u32[]{:S(2)}) copy-start(f32[16,512]{1,0:T(8,128)} %param.21) | copy-start | bytes 98308
  44.0 138.9 %all-gather.5.cloned.1.call-start = ((), (), s32[]{:S(2)}) async-start(), calls=%async_computation.3 | async-start | bytes 2506752 | tf_op jit(solution)/shard_map/all_gather | solution.py:76
  208.1 3.5 copy-start.2
  819.4 5.2 copy-start.8
  819.4 97.7 %all-to-all-start.1 = ((bf16[16,256,512]{2,1,0:T(8,128)(2,1)}), bf16[16,256,512]{2,1,0:T(8,128)(2,1)}, u32[]{:S(2)}, u32[]{:S(2)}) async-start(bf16[16,256,512]{2,1,0:T(8,128)(2,1)} %bitcast.2230), calls=%async_computation.1 | async-start | bytes 8388608 | tf_op jit(solution)/shard_map/all_to_all | solution.py:137
  933.0 13.7 %copy-start.1 = (bf16[256,512]{1,0:T(8,128)(2,1)S(1)}, bf16[256,512]{1,0:T(8,128)(2,1)}, u32[]{:S(2)}) copy-start(bf16[256,512]{1,0:T(8,128)(2,1)} %param.19) | copy-start | bytes 786436
Sparse Core Ops, SparseCore 0:
  9.5 81.8 all-gather.2
  97.2 64.7 all-gather.4
where the time goes:
time: 973 us; the launch traced here: 954 us
  other arithmetic  487 us (50%)
  local copies, waits for them, and re-layouts  219 us (23%)
  waiting for transfers between devices  199 us (20%)
  starting transfers between devices  14 us (1%)
  between operations  13.6 us (1%)
  matrix products  12.6 us (1%)
    reduce_sum x360, other arithmetic, scan_step(): result = jnp.sum(carry * out_map[:, :, None], axis=1) + skip[None] * signal  169 us
    mul x160, other arithmetic, scan_step(): step * signal  123 us
    slice x80, local copies, waits for them, and re-layouts, advance(): conv_piece[inner]  121 us
    all_to_all x1, waiting for transfers between devices, body(): lax.all_to_all(shortened(scanned_chan), 'dp', split_axis=0, concat_axis=1...  85.9 us
    all_to_all x1, waiting for transfers between devices, body(): lax.all_to_all(convolved, 'dp', split_axis=1, concat_axis=0, tiled=True)  65 us
    convert_element_type x80, other arithmetic, scan_step(): step = delta_now.astype(jnp.float32)  64.4 us
    all_gather x1, waiting for transfers between devices, body(): lax.all_gather(x_weight, 'dp', axis=0, tiled=True)  47.4 us
    convert_element_type x640, other arithmetic, scan_step(): out_map = maps_now[:, width:].astype(jnp.float32)  47.3 us
  transfers between devices with their start and end apart: 5, of which 3 were waited for; matrix products, arithmetic and copies ran while one was open for 6% of the time, Pallas kernels for 0%

commit v1 on v0

v1 whole, which is shorter than its diff:
```python
import jax
import jax.numpy as jnp
from jax import lax
from jax.experimental import pallas as pl
from jax.experimental.pallas import tpu as pltpu
from jax.sharding import PartitionSpec as P

BLK = 128
SUB = 8
LANE = 128
HALO = 8
LOG2E = 1.4426950408889634
VMEM_LIMIT = 48 * 1024 * 1024


def passed_along(block, axis, distance):
    devices = range(lax.axis_size(axis))
    route = [(i - distance, i) for i in devices if i - distance in devices]
    return lax.ppermute(block, axis, route)


def params():
    return pltpu.CompilerParams(vmem_limit_bytes=VMEM_LIMIT)


def conv_kernel(first_ref, x_ref, halo_ref, w_ref, b_ref, out_ref):
    taps = w_ref.shape[0]
    w = w_ref[...].astype(jnp.float32)
    bias = b_ref[...].astype(jnp.float32)
    chans = x_ref.shape[1]
    row = lax.broadcasted_iota(jnp.int32, (SUB, chans), 0)
    before = halo_ref[...].astype(jnp.float32)
    for blk in range(x_ref.shape[0] // BLK):
        now = x_ref[blk * BLK : (blk + 1) * BLK, :].astype(jnp.float32)
        before = jnp.where(first_ref[blk] == 0, before, 0.0)
        acc = now * w[taps - 1 : taps] + bias
        for back in range(1, taps):
            rolled = pltpu.roll(now, back, 0)
            head = jnp.where(row < back, pltpu.roll(before, back, 0), rolled[:SUB])
            shifted = jnp.concatenate([head, rolled[SUB:]], 0)
            acc = acc + shifted * w[taps - 1 - back : taps - back]
        out_ref[0, blk * BLK : (blk + 1) * BLK, :] = jax.nn.silu(acc).astype(jnp.bfloat16)
        before = now[BLK - SUB :]


def proj_kernel(conv_ref, w_ref, out_ref, acc_ref):
    step = pl.program_id(0)

    @pl.when(step == 0)
    def _():
        acc_ref[...] = jnp.zeros_like(acc_ref)

    acc_ref[...] += jnp.dot(conv_ref[0], w_ref[...], preferred_element_type=jnp.float32)

    @pl.when(step == pl.num_programs(0) - 1)
    def _():
        out_ref[...] = acc_ref[...].astype(jnp.bfloat16)


def scan_kernel(
    first_ref, conv_ref, proj_ref, dtw_ref, dtb_ref, alog_ref, skip_ref, out_ref,
    carry_ref, rate_ref, delta_ref, drive_ref, maps_ref, part_ref,
):
    step = pl.program_id(0)
    state, chans = alog_ref.shape
    rank = dtw_ref.shape[0]

    @pl.when(step == 0)
    def _():
        rate_ref[...] = jnp.exp(alog_ref[...]) * (-LOG2E)
        carry_ref[...] = jnp.zeros_like(carry_ref)

    @pl.when(first_ref[step] != 0)
    def _():
        carry_ref[...] = jnp.zeros_like(carry_ref)

    signal = conv_ref[...].astype(jnp.float32)
    summed = jnp.dot(proj_ref[:, :rank], dtw_ref[...], preferred_element_type=jnp.float32)
    delta = jax.nn.softplus(summed + dtb_ref[...].astype(jnp.float32))
    delta = delta.astype(jnp.bfloat16).astype(jnp.float32)
    delta_ref[...] = delta
    drive_ref[...] = delta * signal

    maps = proj_ref[:, rank:].astype(jnp.float32)
    pairs = maps.shape[1]
    spread = jnp.broadcast_to(maps[:, None, :], (BLK, state, pairs))
    place = lax.broadcasted_iota(jnp.int32, (BLK, state, pairs), 1)
    column = lax.broadcasted_iota(jnp.int32, (BLK, state, pairs), 2)
    keep = (column == place) | (column == place + state)
    spread = jnp.where(keep, spread, 0.0).reshape(BLK * state, pairs).astype(jnp.bfloat16)
    up = lax.broadcasted_iota(jnp.int32, (pairs, 2 * LANE), 0) < state
    left = lax.broadcasted_iota(jnp.int32, (pairs, 2 * LANE), 1) < LANE
    ones = jnp.where(up == left, 1.0, 0.0).astype(jnp.bfloat16)
    maps_ref[...] = jnp.dot(spread, ones, preferred_element_type=jnp.float32)

    halves = state // SUB
    tiles = chans // LANE
    rates = [
        [rate_ref[n * SUB : (n + 1) * SUB, c * LANE : (c + 1) * LANE] for c in range(tiles)]
        for n in range(halves)
    ]
    first = tuple(
        carry_ref[n * SUB : (n + 1) * SUB, c * LANE : (c + 1) * LANE]
        for n in range(halves)
        for c in range(tiles)
    )

    def advance(group, carry):
        carry = list(carry)
        rows = pl.ds(pl.multiple_of(group * SUB, SUB), SUB)
        deltas = delta_ref[rows, :]
        drives = drive_ref[rows, :]
        for inner in range(SUB):
            t = group * SUB + inner
            base = pl.multiple_of(t * state, state)
            in_map = [maps_ref[pl.ds(base + n * SUB, SUB), :LANE] for n in range(halves)]
            out_map = [maps_ref[pl.ds(base + n * SUB, SUB), LANE:] for n in range(halves)]
            for c in range(tiles):
                lanes = slice(c * LANE, (c + 1) * LANE)
                now = jnp.broadcast_to(deltas[inner : inner + 1, lanes], (SUB, LANE))
                drive = jnp.broadcast_to(drives[inner : inner + 1, lanes], (SUB, LANE))
                total = None
                for n in range(halves):
                    h = jnp.exp2(now * rates[n][c]) * carry[n * tiles + c] + drive * in_map[n]
                    carry[n * tiles + c] = h
                    total = h * out_map[n] if total is None else total + h * out_map[n]
                part_ref[c, pl.ds(pl.multiple_of(t * SUB, SUB), SUB), :] = total
        return tuple(carry)

    last = lax.fori_loop(0, BLK // SUB, advance, first)
    for n in range(halves):
        for c in range(tiles):
            carry_ref[n * SUB : (n + 1) * SUB, c * LANE : (c + 1) * LANE] = last[n * tiles + c]

    total = skip_ref[...] * conv_ref[...].astype(jnp.float32)
    for k in range(SUB):
        parts = [part_ref[c, pl.ds(k, BLK, stride=SUB), :] for c in range(tiles)]
        total = total + jnp.concatenate(parts, 1)
    out_ref[...] = total.astype(jnp.bfloat16)


def gate_kernel(live_ref, scanned_ref, gate_ref, out_ref):
    row = lax.broadcasted_iota(jnp.int32, (BLK, gate_ref.shape[1]), 0)
    for blk in range(gate_ref.shape[0] // BLK):
        rows = slice(blk * BLK, (blk + 1) * BLK)
        gated = scanned_ref[0, rows, :].astype(jnp.float32) * jax.nn.silu(
            gate_ref[rows, :].astype(jnp.float32)
        )
        out_ref[rows, :] = jnp.where(row < live_ref[blk], gated, 0.0).astype(jnp.bfloat16)


def body(
    mixer_in,
    gate_in,
    conv_weight,
    conv_bias,
    x_weight,
    dt_weight,
    dt_bias,
    a_log,
    d_skip,
    block_slot,
    block_first,
    block_live,
):
    ndev = lax.axis_size("dp")
    device = lax.axis_index("dp")
    tok_dev, width = mixer_in.shape
    taps = conv_weight.shape[0]
    state, chans = a_log.shape
    rank = dt_weight.shape[0]
    cols = x_weight.shape[1]
    per_dev = tok_dev // BLK
    total_tok = tok_dev * ndev
    local_first = lax.dynamic_slice_in_dim(block_first, device * per_dev, per_dev)
    local_live = lax.dynamic_slice_in_dim(block_live, device * per_dev, per_dev)
    x_all = lax.all_gather(x_weight, "dp", axis=0, tiled=True)
    halo = passed_along(mixer_in[tok_dev - HALO :], "dp", 1)
    smem = pl.BlockSpec(memory_space=pltpu.SMEM)

    convolved = pl.pallas_call(
        conv_kernel,
        grid=(ndev,),
        in_specs=[
            smem,
            pl.BlockSpec((tok_dev, chans), lambda i: (0, i)),
            pl.BlockSpec((HALO, chans), lambda i: (0, i)),
            pl.BlockSpec((taps, chans), lambda i: (0, i)),
            pl.BlockSpec((1, chans), lambda i: (0, i)),
        ],
        out_specs=pl.BlockSpec((1, tok_dev, chans), lambda i: (i, 0, 0)),
        out_shape=jax.ShapeDtypeStruct((ndev, tok_dev, chans), jnp.bfloat16),
        compiler_params=params(),
        cost_estimate=pl.CostEstimate(
            flops=20 * tok_dev * width, bytes_accessed=4 * tok_dev * width, transcendentals=0
        ),
        name="conv",
    )(local_first, mixer_in, halo, conv_weight, conv_bias[None])

    conv_chan = lax.all_to_all(convolved, "dp", split_axis=0, concat_axis=0, tiled=True)

    proj = pl.pallas_call(
        proj_kernel,
        grid=(ndev,),
        in_specs=[
            pl.BlockSpec((1, tok_dev, chans), lambda i: (i, 0, 0)),
            pl.BlockSpec((chans, cols), lambda i: (i, 0)),
        ],
        out_specs=pl.BlockSpec((tok_dev, cols), lambda i: (0, 0)),
        out_shape=jax.ShapeDtypeStruct((tok_dev, cols), jnp.bfloat16),
        scratch_shapes=[pltpu.VMEM((tok_dev, cols), jnp.float32)],
        compiler_params=params(),
        cost_estimate=pl.CostEstimate(
            flops=2 * tok_dev * width * cols,
            bytes_accessed=2 * (tok_dev + cols) * width,
            transcendentals=0,
        ),
        name="proj",
    )(convolved, x_all)
    proj_all = lax.all_gather(proj, "dp", axis=0, tiled=True)

    whole = lambda a, b: pl.BlockSpec((a, b), lambda i: (0, 0))
    scanned_chan = pl.pallas_call(
        scan_kernel,
        grid=(total_tok // BLK,),
        in_specs=[
            smem,
            pl.BlockSpec((BLK, chans), lambda i: (i, 0)),
            pl.BlockSpec((BLK, cols), lambda i: (i, 0)),
            whole(rank, chans),
            whole(1, chans),
            whole(state, chans),
            whole(1, chans),
        ],
        out_specs=pl.BlockSpec((BLK, chans), lambda i: (i, 0)),
        out_shape=jax.ShapeDtypeStruct((total_tok, chans), jnp.bfloat16),
        scratch_shapes=[
            pltpu.VMEM((state, chans), jnp.float32),
            pltpu.VMEM((state, chans), jnp.float32),
            pltpu.VMEM((BLK, chans), jnp.float32),
            pltpu.VMEM((BLK, chans), jnp.float32),
            pltpu.VMEM((BLK * state, 2 * LANE), jnp.float32),
            pltpu.VMEM((chans // LANE, BLK * SUB, LANE), jnp.float32),
        ],
        compiler_params=params(),
        name="scan",
    )(
        block_first,
        conv_chan.reshape(total_tok, chans),
        proj_all,
        dt_weight,
        dt_bias[None],
        a_log,
        d_skip[None],
    )

    scanned = lax.all_to_all(
        scanned_chan.reshape(ndev, tok_dev, chans), "dp", split_axis=0, concat_axis=0, tiled=True
    )
    return pl.pallas_call(
        gate_kernel,
        grid=(ndev,),
        in_specs=[
            smem,
            pl.BlockSpec((1, tok_dev, chans), lambda i: (i, 0, 0)),
            pl.BlockSpec((tok_dev, chans), lambda i: (0, i)),
        ],
        out_specs=pl.BlockSpec((tok_dev, chans), lambda i: (0, i)),
        out_shape=jax.ShapeDtypeStruct((tok_dev, width), jnp.bfloat16),
        compiler_params=params(),
        name="gate",
    )(local_live, scanned, gate_in)


def solution(mesh):
    in_specs = (
        P(("parts", "dp"), None),
        P(("parts", "dp"), None),
        P(),
        P(),
        P("dp", None),
        P(None, "dp"),
        P("dp"),
        P(None, "dp"),
        P("dp"),
        P("parts"),
        P("parts"),
        P("parts"),
    )
    out_specs = P(("parts", "dp"), None)
    return jax.shard_map(body, mesh=mesh, in_specs=in_specs, out_specs=out_specs, check_vma=False)
```

time: 973 us -> 371 us (0.38); the launches traced: 954 us -> 370 us
  other arithmetic: 487 us -> 0 us
  local copies, waits for them, and re-layouts: 219 us -> 11.3 us
  Pallas kernels: 0 us -> 101 us
  waiting for transfers between devices: 199 us -> 227 us
  matrix products: 12.6 us -> 0 us
    reduce_sum x360 -> x0, other arithmetic: 169 us -> none  [scan_step(): result = jnp.sum(carry * out_map[:, :, None], axis=1) + skip[None] * signal]
    convert_element_type x727 -> x0, other arithmetic: 143 us -> none  [the longest x80 64.4 us: scan_step(): step = delta_now.astype(jnp.float32)]
    mul x161 -> x0, other arithmetic: 124 us -> none  [the longest x160 123 us: scan_step(): step * signal]
    slice x81 -> x1, local copies, waits for them, and re-layouts: 122 us -> 0.92 us  [body(): halo = passed_along(mixer_in[tok_dev - HALO:], 'dp', 1)]
    pallas_call x0 -> x4, Pallas kernels: none -> 101 us  [the longest x1 66.9 us: body(): pl.pallas_call(scan_kernel, grid=(total_tok // BLK,), in_specs=[smem, pl....]
    sub x80 -> x0, other arithmetic: 28.6 us -> none  [scan_step(): 1.0 - start_now]
    all_gather x1, waiting for transfers between devices: 0.01 us -> 24 us  [body(): proj_all = lax.all_gather(proj, 'dp', axis=0, tiled=True)]
    all_gather x1, waiting for transfers between devices: 47.4 us -> 70 us  [body(): x_all = lax.all_gather(x_weight, 'dp', axis=0, tiled=True)]
  transfers between devices with their start and end apart: 5 -> 5, of which waited for: 3 -> 5; matrix products, arithmetic and copies ran while one was open for 6% -> 1% of each run, Pallas kernels for 0% -> 6%
where the time goes in v1:
time: 371 us; the launch traced here: 370 us
  waiting for transfers between devices  227 us (61%)
  Pallas kernels  101 us (27%)
  starting transfers between devices  16.5 us (4%)
  between operations  13.5 us (4%)
  local copies, waits for them, and re-layouts  11.3 us (3%)
    all_to_all x1, waiting for transfers between devices, body(): lax.all_to_all(scanned_chan.reshape(ndev, tok_dev, chans), 'dp', split_ax...  92.4 us
    all_gather x1, waiting for transfers between devices, body(): x_all = lax.all_gather(x_weight, 'dp', axis=0, tiled=True)  70 us
    pallas_call x1, Pallas kernels, body(): pl.pallas_call(scan_kernel, grid=(total_tok // BLK,), in_specs=[smem, pl....  66.9 us
    all_to_all x1, waiting for transfers between devices, body(): lax.all_to_all(convolved, 'dp', split_axis=0, concat_axis=0, tiled=True)  40.1 us
    all_gather x1, waiting for transfers between devices, body(): proj_all = lax.all_gather(proj, 'dp', axis=0, tiled=True)  24 us
    pallas_call x1, Pallas kernels, body(): pl.pallas_call(gate_kernel, grid=(ndev,), in_specs=[smem, pl.BlockSpec((1...  11.8 us
    pallas_call x1, Pallas kernels, body(): pl.pallas_call(proj_kernel, grid=(ndev,), in_specs=[pl.BlockSpec((1, tok_...  11.7 us
    pallas_call x1, Pallas kernels, body(): pl.pallas_call(conv_kernel, grid=(ndev,), in_specs=[smem, pl.BlockSpec((t...  11.1 us
  transfers between devices with their start and end apart: 5, of which 5 were waited for; matrix products, arithmetic and copies ran while one was open for 1% of the time, Pallas kernels for 6%

profile of v1, /device:TPU:13, one launch (start us, length us, event | category | flops | bytes accessed | tf_op | source)
XLA Modules:
  0.0 369.7 jit_solution(1231114744621227702)
XLA Ops:
  6.5 0.0 all-gather.3.cloned.1.call-start
  6.5 1.9 copy.12
  8.4 0.0 all-gather.3.cloned.1.call-update
  8.4 0.9 slice.3
  9.4 3.7 %collective-permute-start = (bf16[8,8192]{1,0:T(8,128)(2,1)S(1)}, bf16[8,8192]{1,0:T(8,128)(2,1)S(1)}, u32[]{:S(2)}, u32[]{:S(2)}) collective-permute-start(bf16[8,8192]{1,0:T(8,128)(2,1)S(1)} %slice.3), channel_id=1, source_target_pairs={{0,1},{1,2},{2,3},{3,4},{4,5},{5,6},{6,7},{7,8},{8,9},{9,10},{10,1... | collective-permute-start | bytes 393224 | tf_op jit(solution)/shard_map/ppermute | solution.py:19
  13.1 0.7 broadcast_in_dim.9.b_ref
  13.8 0.7 dynamic_slice.7.first_ref
  14.6 0.4 collective-permute-done.halo_ref
  15.0 0.0 copy-start.4
  15.0 0.8 copy-done.4
  15.8 11.1 %conv.1.conv_ref = bf16[16,256,512]{2,1,0:T(8,128)(2,1)S(1)} custom-call(s32[2]{0:T(128)S(1)} %dynamic_slice.7.first_ref, bf16[256,8192]{1,0:T(8,128)(2,1)} %x_ref.1, bf16[8,8192]{1,0:T(8,128)(2,1)S(1)} %collective-permute-done.halo_ref, bf16[4,8192]{1,0:T(4,128)(2,1)S(1)} %copy-done.4, bf16[1,8192]{1,0:T(2,128)(2,1)S(1)} %broadcast_in_dim.9.b_ref), custom_call_target="tpu_custom_call" | custom-call | flops 41943040 | bytes 8388608 | tf_op jit(solution)/shard_map/conv/pallas_call | solution.py:181
  26.9 0.0 copy-start
  27.0 2.0 copy-done
  29.0 0.0 copy-start.8
  29.0 0.0 copy-start.3
  29.0 0.0 copy-start.5
  29.0 0.0 copy-start.6
  29.0 0.0 copy-start.7
  29.0 7.4 %all-to-all-start = ((bf16[16,256,512]{2,1,0:T(8,128)(2,1)}), bf16[16,256,512]{2,1,0:T(8,128)(2,1)}, u32[]{:S(2)}, u32[]{:S(2)}) async-start(bf16[16,256,512]{2,1,0:T(8,128)(2,1)} %copy-done), calls=%async_computation | async-start | bytes 8388608 | tf_op jit(solution)/shard_map/all_to_all | solution.py:200
  36.3 0.0 all-gather.5.cloned.1.call-start
  36.4 70.0 %all-gather.3.cloned.1.call-done.w_ref = bf16[8192,288]{1,0:T(8,128)(2,1)} async-done(((bf16[512,288]{1,0:T(8,128)(2,1)}), bf16[8192,288]{1,0:T(8,128)(2,1)}) %all-gather.3.cloned.1.call-update) | async-done | bytes 4718608 | tf_op jit(solution)/shard_map/all_gather | solution.py:177
  106.4 0.0 copy-start.1
  106.4 2.2 copy-done.1
  108.6 11.7 %proj.1 = bf16[256,288]{1,0:T(8,128)(2,1)} custom-call(bf16[16,256,512]{2,1,0:T(8,128)(2,1)S(1)} %copy-done.1, bf16[8192,288]{1,0:T(8,128)(2,1)} %all-gather.3.cloned.1.call-done.w_ref), custom_call_target="tpu_custom_call" | custom-call | flops 1207959552 | bytes 8912896 | tf_op jit(solution)/shard_map/proj/pallas_call | solution.py:202
  120.2 0.0 all-gather.5.cloned.1.call-update
  120.2 0.0 copy-done.8
  120.3 40.1 %all-to-all-done = bf16[16,256,512]{2,1,0:T(8,128)(2,1)} async-done(((bf16[16,256,512]{2,1,0:T(8,128)(2,1)}), bf16[16,256,512]{2,1,0:T(8,128)(2,1)}, u32[]{:S(2)}, u32[]{:S(2)}) %all-to-all-start) | async-done | bytes 4194336 | tf_op jit(solution)/shard_map/all_to_all | solution.py:200
  160.4 24.0 %all-gather.5.cloned.1.call-done.proj_ref = bf16[4096,288]{1,0:T(8,128)(2,1)} async-done(((bf16[256,288]{1,0:T(8,128)(2,1)}), bf16[4096,288]{1,0:T(8,128)(2,1)}) %all-gather.5.cloned.1.call-update) | async-done | bytes 2359312 | tf_op jit(solution)/shard_map/all_gather | solution.py:220
  184.4 0.0 copy-done.3
  184.4 0.0 copy-done.5
  184.4 0.0 copy-done.6
  184.4 0.0 copy-done.7
  184.4 0.0 copy-start.2
  184.4 1.9 copy-done.2
  186.3 66.9 %scan.1 = bf16[4096,512]{1,0:T(8,128)(2,1)} custom-call(s32[32]{0:T(128)S(1)} %copy-done.7, bf16[4096,512]{1,0:T(8,128)(2,1)} %bitcast.conv_ref, bf16[4096,288]{1,0:T(8,128)(2,1)S(1)} %copy-done.2, bf16[256,512]{1,0:T(8,128)(2,1)S(1)} %copy-done.3, bf16[1,512]{1,0:T(2,128)(2,1)S(1)} %broadcast_in_dim.10.dtb_ref, f32[16,512]{1,0:T(8,128)S(1)} %copy-done.5, ...), custom_call_target="tpu_custom_call" | custom-call | tf_op jit(solution)/shard_map/scan/pallas_call | solution.py:223
  253.2 0.0 copy-start.9
  253.2 5.4 %all-to-all-start.1 = ((bf16[16,256,512]{2,1,0:T(8,128)(2,1)}), bf16[16,256,512]{2,1,0:T(8,128)(2,1)}, u32[]{:S(2)}, u32[]{:S(2)}) async-start(bf16[16,256,512]{2,1,0:T(8,128)(2,1)} %bitcast.4), calls=%async_computation.1 | async-start | bytes 8388608 | tf_op jit(solution)/shard_map/all_to_all | solution.py:257
  258.5 0.0 copy-done.9
  258.6 0.1 dynamic_slice.6.live_ref
  258.6 92.4 %all-to-all-done.1.scanned_ref = bf16[16,256,512]{2,1,0:T(8,128)(2,1)} async-done(((bf16[16,256,512]{2,1,0:T(8,128)(2,1)}), bf16[16,256,512]{2,1,0:T(8,128)(2,1)}, u32[]{:S(2)}, u32[]{:S(2)}) %all-to-all-start.1) | async-done | bytes 4194336 | tf_op jit(solution)/shard_map/all_to_all | solution.py:257
  351.0 11.8 %gate.1 = bf16[256,8192]{1,0:T(8,128)(2,1)} custom-call(s32[2]{0:T(128)S(1)} %dynamic_slice.6.live_ref, bf16[16,256,512]{2,1,0:T(8,128)(2,1)} %all-to-all-done.1.scanned_ref, bf16[256,8192]{1,0:T(8,128)(2,1)} %gate_ref.1), custom_call_target="tpu_custom_call" | custom-call | tf_op jit(solution)/shard_map/gate/pallas_call | solution.py:260
  (1 shorter events, 0.0 us)
Async XLA Ops:
  6.5 99.8 %all-gather.3.cloned.1.call-start = ((), (), s32[]{:S(2)}) async-start(), calls=%async_computation.2 | async-start | bytes 6684672 | tf_op jit(solution)/shard_map/all_gather | solution.py:177
  9.4 5.6 %collective-permute-start = (bf16[8,8192]{1,0:T(8,128)(2,1)S(1)}, bf16[8,8192]{1,0:T(8,128)(2,1)S(1)}, u32[]{:S(2)}, u32[]{:S(2)}) collective-permute-start(bf16[8,8192]{1,0:T(8,128)(2,1)S(1)} %slice.3), channel_id=1, source_target_pairs={{0,1},{1,2},{2,3},{3,4},{4,5},{5,6},{6,7},{7,8},{8,9},{9,10},{10,1... | collective-permute-start | bytes 393224 | tf_op jit(solution)/shard_map/ppermute | solution.py:19
  15.0 0.8 copy-start.4
  26.9 2.0 copy-start
  29.0 91.3 %copy-start.8 = (bf16[512]{0:T(512)(128)(2,1)S(1)}, bf16[512]{0:T(512)(128)(2,1)}, u32[]{:S(2)}) copy-start(bf16[512]{0:T(512)(128)(2,1)} %param.18) | copy-start | bytes 3076
  29.0 155.4 %copy-start.3 = (bf16[256,512]{1,0:T(8,128)(2,1)S(1)}, bf16[256,512]{1,0:T(8,128)(2,1)}, u32[]{:S(2)}) copy-start(bf16[256,512]{1,0:T(8,128)(2,1)} %dtw_ref.1) | copy-start | bytes 786436
  29.0 155.4 %copy-start.5 = (f32[16,512]{1,0:T(8,128)S(1)}, f32[16,512]{1,0:T(8,128)}, u32[]{:S(2)}) copy-start(f32[16,512]{1,0:T(8,128)} %alog_ref.1) | copy-start | bytes 98308
  29.0 155.4 %copy-start.6 = (f32[512]{0:T(512)S(1)}, f32[512]{0:T(512)}, u32[]{:S(2)}) copy-start(f32[512]{0:T(512)} %param.20) | copy-start | bytes 6148
  29.0 155.4 %copy-start.7 = (s32[32]{0:T(128)S(1)}, s32[32]{0:T(128)}, u32[]{:S(2)}) copy-start(s32[32]{0:T(128)} %first_ref.1) | copy-start | bytes 388
  29.0 131.4 %all-to-all-start = ((bf16[16,256,512]{2,1,0:T(8,128)(2,1)}), bf16[16,256,512]{2,1,0:T(8,128)(2,1)}, u32[]{:S(2)}, u32[]{:S(2)}) async-start(bf16[16,256,512]{2,1,0:T(8,128)(2,1)} %copy-done), calls=%async_computation | async-start | bytes 8388608 | tf_op jit(solution)/shard_map/all_to_all | solution.py:200
  36.3 148.1 %all-gather.5.cloned.1.call-start = ((), (), s32[]{:S(2)}) async-start(), calls=%async_computation.3 | async-start | bytes 3342336 | tf_op jit(solution)/shard_map/all_gather | solution.py:220
  106.4 2.2 copy-start.1
  184.4 1.9 copy-start.2
  253.2 5.4 %copy-start.9 = (s32[32]{0:T(128)S(1)}, s32[32]{0:T(128)}, u32[]{:S(2)}) copy-start(s32[32]{0:T(128)} %param.22) | copy-start | bytes 388
  253.2 97.9 %all-to-all-start.1 = ((bf16[16,256,512]{2,1,0:T(8,128)(2,1)}), bf16[16,256,512]{2,1,0:T(8,128)(2,1)}, u32[]{:S(2)}, u32[]{:S(2)}) async-start(bf16[16,256,512]{2,1,0:T(8,128)(2,1)} %bitcast.4), calls=%async_computation.1 | async-start | bytes 8388608 | tf_op jit(solution)/shard_map/all_to_all | solution.py:257
Sparse Core Ops, SparseCore 0:
  9.6 96.6 all-gather.2
  120.4 64.0 all-gather.4

commit v2 on v1

--- a/solution.py
+++ b/solution.py
@@ -1,3 +1,5 @@
+import functools
+
 import jax
 import jax.numpy as jnp
 from jax import lax
@@ -43,18 +45,10 @@
         before = now[BLK - SUB :]
 
 
-def proj_kernel(conv_ref, w_ref, out_ref, acc_ref):
-    step = pl.program_id(0)
-
-    @pl.when(step == 0)
-    def _():
-        acc_ref[...] = jnp.zeros_like(acc_ref)
-
-    acc_ref[...] += jnp.dot(conv_ref[0], w_ref[...], preferred_element_type=jnp.float32)
-
-    @pl.when(step == pl.num_programs(0) - 1)
-    def _():
-        out_ref[...] = acc_ref[...].astype(jnp.bfloat16)
+def proj_kernel(conv_ref, w_ref, out_ref):
+    out_ref[0] = jnp.dot(conv_ref[0], w_ref[...], preferred_element_type=jnp.float32).astype(
+        jnp.bfloat16
+    )
 
 
 def scan_kernel(
@@ -139,14 +133,19 @@
     out_ref[...] = total.astype(jnp.bfloat16)
 
 
-def gate_kernel(live_ref, scanned_ref, gate_ref, out_ref):
-    row = lax.broadcasted_iota(jnp.int32, (BLK, gate_ref.shape[1]), 0)
+def gate_kernel(pieces, live_ref, *refs):
+    gate_ref, out_ref = refs[pieces:]
+    chans = refs[0].shape[2]
+    row = lax.broadcasted_iota(jnp.int32, (BLK, chans), 0)
     for blk in range(gate_ref.shape[0] // BLK):
         rows = slice(blk * BLK, (blk + 1) * BLK)
-        gated = scanned_ref[0, rows, :].astype(jnp.float32) * jax.nn.silu(
-            gate_ref[rows, :].astype(jnp.float32)
-        )
-        out_ref[rows, :] = jnp.where(row < live_ref[blk], gated, 0.0).astype(jnp.bfloat16)
+        for piece in range(pieces):
+            lanes = slice(piece * chans, (piece + 1) * chans)
+            gated = refs[piece][0, rows, :].astype(jnp.float32) * jax.nn.silu(
+                gate_ref[rows, lanes].astype(jnp.float32)
+            )
+            gated = jnp.where(row < live_ref[blk], gated, 0.0)
+            out_ref[rows, lanes] = gated.astype(jnp.bfloat16)
 
 
 def body(
@@ -174,7 +173,6 @@
     total_tok = tok_dev * ndev
     local_first = lax.dynamic_slice_in_dim(block_first, device * per_dev, per_dev)
     local_live = lax.dynamic_slice_in_dim(block_live, device * per_dev, per_dev)
-    x_all = lax.all_gather(x_weight, "dp", axis=0, tiled=True)
     halo = passed_along(mixer_in[tok_dev - HALO :], "dp", 1)
     smem = pl.BlockSpec(memory_space=pltpu.SMEM)
 
@@ -199,77 +197,87 @@
 
     conv_chan = lax.all_to_all(convolved, "dp", split_axis=0, concat_axis=0, tiled=True)
 
-    proj = pl.pallas_call(
+    shares = pl.pallas_call(
         proj_kernel,
         grid=(ndev,),
         in_specs=[
             pl.BlockSpec((1, tok_dev, chans), lambda i: (i, 0, 0)),
-            pl.BlockSpec((chans, cols), lambda i: (i, 0)),
+            pl.BlockSpec((chans, cols), lambda i: (0, 0)),
         ],
-        out_specs=pl.BlockSpec((tok_dev, cols), lambda i: (0, 0)),
-        out_shape=jax.ShapeDtypeStruct((tok_dev, cols), jnp.bfloat16),
-        scratch_shapes=[pltpu.VMEM((tok_dev, cols), jnp.float32)],
+        out_specs=pl.BlockSpec((1, tok_dev, cols), lambda i: (i, 0, 0)),
+        out_shape=jax.ShapeDtypeStruct((ndev, tok_dev, cols), jnp.bfloat16),
         compiler_params=params(),
-        cost_estimate=pl.CostEstimate(
-            flops=2 * tok_dev * width * cols,
-            bytes_accessed=2 * (tok_dev + cols) * width,
-            transcendentals=0,
-        ),
         name="proj",
-    )(convolved, x_all)
-    proj_all = lax.all_gather(proj, "dp", axis=0, tiled=True)
-
-    whole = lambda a, b: pl.BlockSpec((a, b), lambda i: (0, 0))
-    scanned_chan = pl.pallas_call(
-        scan_kernel,
-        grid=(total_tok // BLK,),
-        in_specs=[
-            smem,
-            pl.BlockSpec((BLK, chans), lambda i: (i, 0)),
-            pl.BlockSpec((BLK, cols), lambda i: (i, 0)),
-            whole(rank, chans),
-            whole(1, chans),
-            whole(state, chans),
-            whole(1, chans),
-        ],
-        out_specs=pl.BlockSpec((BLK, chans), lambda i: (i, 0)),
-        out_shape=jax.ShapeDtypeStruct((total_tok, chans), jnp.bfloat16),
-        scratch_shapes=[
-            pltpu.VMEM((state, chans), jnp.float32),
-            pltpu.VMEM((state, chans), jnp.float32),
-            pltpu.VMEM((BLK, chans), jnp.float32),
-            pltpu.VMEM((BLK, chans), jnp.float32),
-            pltpu.VMEM((BLK * state, 2 * LANE), jnp.float32),
-            pltpu.VMEM((chans // LANE, BLK * SUB, LANE), jnp.float32),
-        ],
-        compiler_params=params(),
-        name="scan",
-    )(
-        block_first,
-        conv_chan.reshape(total_tok, chans),
-        proj_all,
-        dt_weight,
-        dt_bias[None],
-        a_log,
-        d_skip[None],
-    )
-
-    scanned = lax.all_to_all(
-        scanned_chan.reshape(ndev, tok_dev, chans), "dp", split_axis=0, concat_axis=0, tiled=True
-    )
+    )(conv_chan, x_weight)
+    shares = lax.all_to_all(shares, "dp", split_axis=0, concat_axis=0, tiled=True)
+    proj = jnp.sum(shares.astype(jnp.float32), axis=0).astype(jnp.bfloat16)
+    proj_all = lax.all_to_all(
+        jnp.broadcast_to(proj[None], (ndev, tok_dev, cols)),
+        "dp",
+        split_axis=0,
+        concat_axis=0,
+        tiled=True,
+    ).reshape(total_tok, cols)
+
+    pieces = 2 if chans % (2 * LANE) == 0 else 1
+    chans = chans // pieces
+    scanned = []
+    for piece in range(pieces):
+        part = lambda a, k=piece: pl.BlockSpec((a, chans), lambda i: (0, k))
+        scanned_chan = pl.pallas_call(
+            scan_kernel,
+            grid=(total_tok // BLK,),
+            in_specs=[
+                smem,
+                pl.BlockSpec((BLK, chans), lambda i, k=piece: (i, k)),
+                pl.BlockSpec((BLK, cols), lambda i: (i, 0)),
+                part(rank),
+                part(1),
+                part(state),
+                part(1),
+            ],
+            out_specs=pl.BlockSpec((BLK, chans), lambda i: (i, 0)),
+            out_shape=jax.ShapeDtypeStruct((total_tok, chans), jnp.bfloat16),
+            scratch_shapes=[
+                pltpu.VMEM((state, chans), jnp.float32),
+                pltpu.VMEM((state, chans), jnp.float32),
+                pltpu.VMEM((BLK, chans), jnp.float32),
+                pltpu.VMEM((BLK, chans), jnp.float32),
+                pltpu.VMEM((BLK * state, 2 * LANE), jnp.float32),
+                pltpu.VMEM((chans // LANE, BLK * SUB, LANE), jnp.float32),
+            ],
+            compiler_params=params(),
+            name="scan",
+        )(
+            block_first,
+            conv_chan.reshape(total_tok, pieces * chans),
+            proj_all,
+            dt_weight,
+            dt_bias[None],
+            a_log,
+            d_skip[None],
+        )
+
+        scanned.append(
+            lax.all_to_all(
+                scanned_chan.reshape(ndev, tok_dev, chans),
+                "dp",
+                split_axis=0,
+                concat_axis=0,
+                tiled=True,
+            )
+        )
     return pl.pallas_call(
-        gate_kernel,
+        functools.partial(gate_kernel, pieces),
         grid=(ndev,),
-        in_specs=[
-            smem,
-            pl.BlockSpec((1, tok_dev, chans), lambda i: (i, 0, 0)),
-            pl.BlockSpec((tok_dev, chans), lambda i: (0, i)),
-        ],
-        out_specs=pl.BlockSpec((tok_dev, chans), lambda i: (0, i)),
+        in_specs=[smem]
+        + [pl.BlockSpec((1, tok_dev, chans), lambda i: (i, 0, 0))] * pieces
+        + [pl.BlockSpec((tok_dev, pieces * chans), lambda i: (0, i))],
+        out_specs=pl.BlockSpec((tok_dev, pieces * chans), lambda i: (0, i)),
         out_shape=jax.ShapeDtypeStruct((tok_dev, width), jnp.bfloat16),
         compiler_params=params(),
         name="gate",
-    )(local_live, scanned, gate_in)
+    )(local_live, *scanned, gate_in)
 
 
 def solution(mesh):

time: 371 us -> 416 us (1.12)
  blocking collectives: 0 us -> 57.8 us
  waiting for transfers between devices: 227 us -> 197 us
  Pallas kernels: 101 us -> 117 us
  between operations: 13.5 us -> 0.18 us
  starting transfers between devices: 16.5 us -> 26.3 us
  local copies, waits for them, and re-layouts: 11.3 us -> 15.9 us
    all_gather x2 -> x0, waiting for transfers between devices: 94 us -> none  [the longest x1 70 us: body(): x_all = lax.all_gather(x_weight, 'dp', axis=0, tiled=True)]
    all_to_all x0 -> x1, blocking collectives: none -> 57.8 us  [body(): lax.all_to_all(shares, 'dp', split_axis=0, concat_axis=0, tiled=True)]
    all_to_all x0 -> x1, waiting for transfers between devices: none -> 53.1 us  [body(): lax.all_to_all(jnp.broadcast_to(proj[None], (ndev, tok_dev, cols)), 'dp',...]
    all_to_all x1, waiting for transfers between devices: 40.1 us -> 92.2 us  [body(): lax.all_to_all(convolved, 'dp', split_axis=0, concat_axis=0, tiled=True)]
    all_to_all x1 -> x2, waiting for transfers between devices: 92.4 us -> 51.6 us  [body(): lax.all_to_all(scanned_chan.reshape(ndev, tok_dev, chans), 'dp', split_ax...]
    pallas_call x1 -> x2, Pallas kernels: 66.9 us -> 84 us  [body(): pl.pallas_call(scan_kernel, grid=(total_tok // BLK,), in_specs=[smem, pl....]
    all_to_all x0 -> x1, starting transfers between devices: none -> 5.51 us  [body(): lax.all_to_all(jnp.broadcast_to(proj[None], (ndev, tok_dev, cols)), 'dp',...]
    all_to_all x1 -> x2, starting transfers between devices: 5.38 us -> 9.78 us  [body(): lax.all_to_all(scanned_chan.reshape(ndev, tok_dev, chans), 'dp', split_ax...]
  transfers between devices with their start and end apart: 5 -> 5, of which waited for: 5 -> 5; matrix products, arithmetic and copies ran while one was open for 1% -> 0% of each run, Pallas kernels for 6% -> 10%
where the time goes in v2:
time: 416 us; the launch traced here: 415 us
  waiting for transfers between devices  197 us (47%)
  Pallas kernels  117 us (28%)
  blocking collectives  57.8 us (14%)
  starting transfers between devices  26.3 us (6%)
  local copies, waits for them, and re-layouts  15.9 us (4%)
    all_to_all x1, waiting for transfers between devices, body(): lax.all_to_all(convolved, 'dp', split_axis=0, concat_axis=0, tiled=True)  92.2 us
    pallas_call x2, Pallas kernels, body(): pl.pallas_call(scan_kernel, grid=(total_tok // BLK,), in_specs=[smem, pl....  84 us
    all_to_all x1, blocking collectives, body(): lax.all_to_all(shares, 'dp', split_axis=0, concat_axis=0, tiled=True)  57.8 us
    all_to_all x1, waiting for transfers between devices, body(): lax.all_to_all(jnp.broadcast_to(proj[None], (ndev, tok_dev, cols)), 'dp',...  53.1 us
    all_to_all x2, waiting for transfers between devices, body(): lax.all_to_all(scanned_chan.reshape(ndev, tok_dev, chans), 'dp', split_ax...  51.6 us
    pallas_call x1, Pallas kernels, body(): pl.pallas_call(functools.partial(gate_kernel, pieces), grid=(ndev,), in_s...  11.7 us
    pallas_call x1, Pallas kernels, body(): pl.pallas_call(conv_kernel, grid=(ndev,), in_specs=[smem, pl.BlockSpec((t...  11.1 us
    pallas_call x1, Pallas kernels, body(): pl.pallas_call(proj_kernel, grid=(ndev,), in_specs=[pl.BlockSpec((1, tok_...  10.4 us
  transfers between devices with their start and end apart: 5, of which 5 were waited for; matrix products, arithmetic and copies ran while one was open for 0% of the time, Pallas kernels for 10%

profile of v2, /device:TPU:13, one launch (start us, length us, event | category | flops | bytes accessed | tf_op | source)
XLA Modules:
  0.0 415.1 jit_solution(6021476840320149364)
XLA Ops:
  0.0 0.9 slice.3
  0.9 3.7 collective-permute-start
  4.6 0.7 broadcast_in_dim.8.b_ref
  5.4 0.7 dynamic_slice.7.first_ref
  6.1 0.4 collective-permute-done.halo_ref
  6.6 0.0 copy-start.5
  6.6 0.8 copy-done.5
  7.4 11.1 %conv.1 = bf16[16,256,512]{2,1,0:T(8,128)(2,1)S(1)} custom-call(s32[2]{0:T(128)S(1)} %dynamic_slice.7.first_ref, bf16[256,8192]{1,0:T(8,128)(2,1)} %x_ref.1, bf16[8,8192]{1,0:T(8,128)(2,1)S(1)} %collective-permute-done.halo_ref, bf16[4,8192]{1,0:T(4,128)(2,1)S(1)} %copy-done.5, bf16[1,8192]{1,0:T(2,128)(2,1)S(1)} %broadcast_in_dim.8.b_ref), custom_call_target="tpu_custom_call" | custom-call | flops 41943040 | bytes 8388608 | tf_op jit(solution)/shard_map/conv/pallas_call | solution.py:179
  18.5 0.0 copy-start
  18.5 2.0 copy-done
  20.5 0.0 copy-start.8
  20.5 7.3 %all-to-all-start = ((bf16[16,256,512]{2,1,0:T(8,128)(2,1)}), bf16[16,256,512]{2,1,0:T(8,128)(2,1)}, u32[]{:S(2)}, u32[]{:S(2)}) async-start(bf16[16,256,512]{2,1,0:T(8,128)(2,1)} %copy-done), calls=%async_computation | async-start | bytes 8388608 | tf_op jit(solution)/shard_map/all_to_all | solution.py:198
  27.8 0.0 copy-done.8
  27.8 0.2 copy.13.w_ref
  28.0 92.2 %all-to-all-done.conv_ref = bf16[16,256,512]{2,1,0:T(8,128)(2,1)} async-done(((bf16[16,256,512]{2,1,0:T(8,128)(2,1)}), bf16[16,256,512]{2,1,0:T(8,128)(2,1)}, u32[]{:S(2)}, u32[]{:S(2)}) %all-to-all-start) | async-done | bytes 4194336 | tf_op jit(solution)/shard_map/all_to_all | solution.py:198
  120.3 10.4 %proj.1 = bf16[16,256,288]{2,1,0:T(8,128)(2,1)S(1)} custom-call(bf16[16,256,512]{2,1,0:T(8,128)(2,1)} %all-to-all-done.conv_ref, bf16[512,288]{1,0:T(8,128)(2,1)S(1)} %copy.13.w_ref), custom_call_target="tpu_custom_call" | custom-call | tf_op jit(solution)/shard_map/proj/pallas_call | solution.py:200
  130.7 2.7 copy.14
  133.5 57.8 %all_to_all.25 = bf16[16,256,288]{1,2,0:T(8,128)(2,1)S(1)} all-to-all(bf16[16,256,288]{1,2,0:T(8,128)(2,1)} %copy.14), channel_id=1, replica_groups=mesh['parts'=2,'dp'=16] {'dp'}, dimensions={0} | all-to-all | bytes 4718592 | tf_op jit(solution)/shard_map/all_to_all | solution.py:212
  191.3 0.3 reduce_sum.12
  191.6 1.6 broadcast_in_dim.18
  193.3 0.0 copy-start.9
  193.3 5.5 %all-to-all-start.2 = ((bf16[16,256,288]{1,2,0:T(8,128)(2,1)}), bf16[16,256,288]{1,2,0:T(8,128)(2,1)}, u32[]{:S(2)}, u32[]{:S(2)}) async-start(bf16[16,256,288]{1,2,0:T(8,128)(2,1)} %broadcast_in_dim.18), calls=%async_computation.2 | async-start | bytes 4718592 | tf_op jit(solution)/shard_map/all_to_all | solution.py:214
  198.8 0.0 copy-done.9
  198.8 0.0 copy-start.3
  198.8 0.0 copy-start.4
  198.8 0.0 copy-start.6
  198.8 0.0 copy-start.7
  198.8 53.1 %all-to-all-done.2 = bf16[16,256,288]{1,2,0:T(8,128)(2,1)} async-done(((bf16[16,256,288]{1,2,0:T(8,128)(2,1)}), bf16[16,256,288]{1,2,0:T(8,128)(2,1)}, u32[]{:S(2)}, u32[]{:S(2)}) %all-to-all-start.2) | async-done | bytes 2359328 | tf_op jit(solution)/shard_map/all_to_all | solution.py:214
  251.9 3.3 copy.15
  255.2 0.0 copy-done.3
  255.3 0.0 copy-done.4
  255.3 0.0 copy-done.6
  255.3 0.0 copy-done.7
  255.3 42.0 %scan.3 = bf16[4096,256]{1,0:T(8,128)(2,1)S(1)} custom-call(s32[32]{0:T(128)S(1)} %copy-done.7, bf16[4096,512]{1,0:T(8,128)(2,1)} %bitcast.conv_ref, bf16[4096,288]{1,0:T(8,128)(2,1)S(1)} %bitcast.5, bf16[256,512]{1,0:T(8,128)(2,1)S(1)} %copy-done.3, bf16[1,512]{1,0:T(2,128)(2,1)S(1)} %broadcast_in_dim.19.dtb_ref, f32[16,512]{1,0:T(8,128)S(1)} %copy-done.4, ...), custom_call_target="tpu_custom_call" | custom-call | tf_op jit(solution)/shard_map/scan/pallas_call | solution.py:227
  297.3 0.0 copy-start.2
  297.3 1.3 copy-done.2
  298.6 4.9 %all-to-all-start.4 = ((bf16[16,256,256]{2,1,0:T(8,128)(2,1)}), bf16[16,256,256]{2,1,0:T(8,128)(2,1)}, u32[]{:S(2)}, u32[]{:S(2)}) async-start(bf16[16,256,256]{2,1,0:T(8,128)(2,1)} %bitcast.8), calls=%async_computation.4 | async-start | bytes 4194304 | tf_op jit(solution)/shard_map/all_to_all | solution.py:262
  303.5 42.0 %scan.2 = bf16[4096,256]{1,0:T(8,128)(2,1)S(1)} custom-call(s32[32]{0:T(128)S(1)} %copy-done.7, bf16[4096,512]{1,0:T(8,128)(2,1)} %bitcast.conv_ref, bf16[4096,288]{1,0:T(8,128)(2,1)S(1)} %bitcast.6, bf16[256,512]{1,0:T(8,128)(2,1)S(1)} %copy-done.3, bf16[1,512]{1,0:T(2,128)(2,1)S(1)} %broadcast_in_dim.19.dtb_ref, f32[16,512]{1,0:T(8,128)S(1)} %copy-done.4, ...), custom_call_target="tpu_custom_call" | custom-call | tf_op jit(solution)/shard_map/scan/pallas_call | solution.py:227
  345.5 0.0 copy-start.1
  345.5 1.3 copy-done.1
  346.8 0.0 copy-start.10
  346.8 4.2 %all-to-all-done.4.refs_1_ = bf16[16,256,256]{2,1,0:T(8,128)(2,1)} async-done(((bf16[16,256,256]{2,1,0:T(8,128)(2,1)}), bf16[16,256,256]{2,1,0:T(8,128)(2,1)}, u32[]{:S(2)}, u32[]{:S(2)}) %all-to-all-start.4) | async-done | bytes 2097184 | tf_op jit(solution)/shard_map/all_to_all | solution.py:262
  351.0 4.9 %all-to-all-start.3 = ((bf16[16,256,256]{2,1,0:T(8,128)(2,1)}), bf16[16,256,256]{2,1,0:T(8,128)(2,1)S(1)}, u32[]{:S(2)}, u32[]{:S(2)}) async-start(bf16[16,256,256]{2,1,0:T(8,128)(2,1)} %bitcast.7), calls=%async_computation.3 | async-start | bytes 4194304 | tf_op jit(solution)/shard_map/all_to_all | solution.py:262
  356.0 0.0 copy-done.10
  356.0 0.1 dynamic_slice.6.live_ref
  356.0 47.3 %all-to-all-done.3.refs_0_ = bf16[16,256,256]{2,1,0:T(8,128)(2,1)S(1)} async-done(((bf16[16,256,256]{2,1,0:T(8,128)(2,1)}), bf16[16,256,256]{2,1,0:T(8,128)(2,1)S(1)}, u32[]{:S(2)}, u32[]{:S(2)}) %all-to-all-start.3) | async-done | bytes 2097184 | tf_op jit(solution)/shard_map/all_to_all | solution.py:262
  403.4 11.7 %gate.1 = bf16[256,8192]{1,0:T(8,128)(2,1)} custom-call(s32[2]{0:T(128)S(1)} %dynamic_slice.6.live_ref, bf16[16,256,256]{2,1,0:T(8,128)(2,1)S(1)} %all-to-all-done.3.refs_0_, bf16[16,256,256]{2,1,0:T(8,128)(2,1)} %all-to-all-done.4.refs_1_, bf16[256,8192]{1,0:T(8,128)(2,1)} %refs_2_.1), custom_call_target="tpu_custom_call" | custom-call | tf_op jit(solution)/shard_map/gate/pallas_call | solution.py:270
  (1 shorter events, 0.0 us)
Async XLA Ops:
  0.9 5.6 %collective-permute-start = (bf16[8,8192]{1,0:T(8,128)(2,1)S(1)}, bf16[8,8192]{1,0:T(8,128)(2,1)S(1)}, u32[]{:S(2)}, u32[]{:S(2)}) collective-permute-start(bf16[8,8192]{1,0:T(8,128)(2,1)S(1)} %slice.3), channel_id=1, source_target_pairs={{0,1},{1,2},{2,3},{3,4},{4,5},{5,6},{6,7},{7,8},{8,9},{9,10},{10,1... | collective-permute-start | bytes 393224 | tf_op jit(solution)/shard_map/ppermute | solution.py:21
  6.6 0.8 copy-start.5
  18.5 2.0 copy-start
  20.5 7.3 %copy-start.8 = (bf16[512,288]{0,1:T(8,128)(2,1)S(1)}, bf16[512,288]{0,1:T(8,128)(2,1)}, u32[]{:S(2)}) copy-start(bf16[512,288]{0,1:T(8,128)(2,1)} %param.16) | copy-start | bytes 884740
  20.5 99.8 %all-to-all-start = ((bf16[16,256,512]{2,1,0:T(8,128)(2,1)}), bf16[16,256,512]{2,1,0:T(8,128)(2,1)}, u32[]{:S(2)}, u32[]{:S(2)}) async-start(bf16[16,256,512]{2,1,0:T(8,128)(2,1)} %copy-done), calls=%async_computation | async-start | bytes 8388608 | tf_op jit(solution)/shard_map/all_to_all | solution.py:198
  193.3 5.5 %copy-start.9 = (bf16[512]{0:T(512)(128)(2,1)S(1)}, bf16[512]{0:T(512)(128)(2,1)}, u32[]{:S(2)}) copy-start(bf16[512]{0:T(512)(128)(2,1)} %param.18) | copy-start | bytes 3076
  193.3 58.7 %all-to-all-start.2 = ((bf16[16,256,288]{1,2,0:T(8,128)(2,1)}), bf16[16,256,288]{1,2,0:T(8,128)(2,1)}, u32[]{:S(2)}, u32[]{:S(2)}) async-start(bf16[16,256,288]{1,2,0:T(8,128)(2,1)} %broadcast_in_dim.18), calls=%async_computation.2 | async-start | bytes 4718592 | tf_op jit(solution)/shard_map/all_to_all | solution.py:214
  198.8 56.5 %copy-start.3 = (bf16[256,512]{1,0:T(8,128)(2,1)S(1)}, bf16[256,512]{1,0:T(8,128)(2,1)}, u32[]{:S(2)}) copy-start(bf16[256,512]{1,0:T(8,128)(2,1)} %dtw_ref.3) | copy-start | bytes 786436
  198.8 56.5 %copy-start.4 = (f32[16,512]{1,0:T(8,128)S(1)}, f32[16,512]{1,0:T(8,128)}, u32[]{:S(2)}) copy-start(f32[16,512]{1,0:T(8,128)} %alog_ref.3) | copy-start | bytes 98308
  198.8 56.5 %copy-start.6 = (f32[512]{0:T(512)S(1)}, f32[512]{0:T(512)}, u32[]{:S(2)}) copy-start(f32[512]{0:T(512)} %param.20) | copy-start | bytes 6148
  198.8 56.5 %copy-start.7 = (s32[32]{0:T(128)S(1)}, s32[32]{0:T(128)}, u32[]{:S(2)}) copy-start(s32[32]{0:T(128)} %first_ref.3) | copy-start | bytes 388
  297.3 1.4 copy-start.2
  298.6 52.4 %all-to-all-start.4 = ((bf16[16,256,256]{2,1,0:T(8,128)(2,1)}), bf16[16,256,256]{2,1,0:T(8,128)(2,1)}, u32[]{:S(2)}, u32[]{:S(2)}) async-start(bf16[16,256,256]{2,1,0:T(8,128)(2,1)} %bitcast.8), calls=%async_computation.4 | async-start | bytes 4194304 | tf_op jit(solution)/shard_map/all_to_all | solution.py:262
  345.5 1.3 copy-start.1
  346.8 9.1 %copy-start.10 = (s32[32]{0:T(128)S(1)}, s32[32]{0:T(128)}, u32[]{:S(2)}) copy-start(s32[32]{0:T(128)} %param.22) | copy-start | bytes 388
  351.0 52.3 %all-to-all-start.3 = ((bf16[16,256,256]{2,1,0:T(8,128)(2,1)}), bf16[16,256,256]{2,1,0:T(8,128)(2,1)S(1)}, u32[]{:S(2)}, u32[]{:S(2)}) async-start(bf16[16,256,256]{2,1,0:T(8,128)(2,1)} %bitcast.7), calls=%async_computation.3 | async-start | bytes 4194304 | tf_op jit(solution)/shard_map/all_to_all | solution.py:262

commit v3 on v1

--- a/solution.py
+++ b/solution.py
@@ -43,14 +43,18 @@
         before = now[BLK - SUB :]
 
 
-def proj_kernel(conv_ref, w_ref, out_ref, acc_ref):
+def proj_kernel(conv_ref, rank_ref, maps_ref, out_ref, acc_ref):
     step = pl.program_id(0)
+    rank = rank_ref.shape[1]
 
     @pl.when(step == 0)
     def _():
         acc_ref[...] = jnp.zeros_like(acc_ref)
 
-    acc_ref[...] += jnp.dot(conv_ref[0], w_ref[...], preferred_element_type=jnp.float32)
+    acc_ref[:, :rank] += jnp.dot(conv_ref[0], rank_ref[...], preferred_element_type=jnp.float32)
+    acc_ref[:, rank:] += lax.dot_general(
+        conv_ref[0], maps_ref[0], (((1,), (1,)), ((), ())), preferred_element_type=jnp.float32
+    )
 
     @pl.when(step == pl.num_programs(0) - 1)
     def _():
@@ -174,7 +178,8 @@
     total_tok = tok_dev * ndev
     local_first = lax.dynamic_slice_in_dim(block_first, device * per_dev, per_dev)
     local_live = lax.dynamic_slice_in_dim(block_live, device * per_dev, per_dev)
-    x_all = lax.all_gather(x_weight, "dp", axis=0, tiled=True)
+    rank_all = lax.all_gather(x_weight[:, :rank], "dp", axis=0, tiled=True)
+    maps_all = lax.all_gather(x_weight[:, rank:].T, "dp", axis=0, tiled=False)
     halo = passed_along(mixer_in[tok_dev - HALO :], "dp", 1)
     smem = pl.BlockSpec(memory_space=pltpu.SMEM)
 
@@ -204,7 +209,8 @@
         grid=(ndev,),
         in_specs=[
             pl.BlockSpec((1, tok_dev, chans), lambda i: (i, 0, 0)),
-            pl.BlockSpec((chans, cols), lambda i: (i, 0)),
+            pl.BlockSpec((chans, rank), lambda i: (i, 0)),
+            pl.BlockSpec((1, cols - rank, chans), lambda i: (i, 0, 0)),
         ],
         out_specs=pl.BlockSpec((tok_dev, cols), lambda i: (0, 0)),
         out_shape=jax.ShapeDtypeStruct((tok_dev, cols), jnp.bfloat16),
@@ -216,7 +222,7 @@
             transcendentals=0,
         ),
         name="proj",
-    )(convolved, x_all)
+    )(convolved, rank_all, maps_all)
     proj_all = lax.all_gather(proj, "dp", axis=0, tiled=True)
 
     whole = lambda a, b: pl.BlockSpec((a, b), lambda i: (0, 0))

time: 371 us -> 401 us (1.081)
  blocking collectives: 0 us -> 120 us
  waiting for transfers between devices: 227 us -> 138 us
    all_gather x0 -> x1, blocking collectives: none -> 120 us  [body(): maps_all = lax.all_gather(x_weight[:, rank:].T, 'dp', axis=0, tiled=False)]
    all_gather x1, waiting for transfers between devices: 70 us -> 0.01 us  [body(): rank_all = lax.all_gather(x_weight[:, :rank], 'dp', axis=0, tiled=True)]
    all_to_all x1, waiting for transfers between devices: 40.1 us -> 0.01 us  [body(): lax.all_to_all(convolved, 'dp', split_axis=0, concat_axis=0, tiled=True)]
    all_gather x1, waiting for transfers between devices: 24 us -> 44.9 us  [body(): proj_all = lax.all_gather(proj, 'dp', axis=0, tiled=True)]
  transfers between devices with their start and end apart: 5 -> 5, of which waited for: 5 -> 3; matrix products, arithmetic and copies ran while one was open for 1% -> 1% of each run, Pallas kernels for 6% -> 6%
where the time goes in v3:
time: 401 us; the launch traced here: 400 us
  waiting for transfers between devices  138 us (34%)
  blocking collectives  120 us (30%)
  Pallas kernels  101 us (25%)
  starting transfers between devices  16.3 us (4%)
  between operations  13.5 us (3%)
  local copies, waits for them, and re-layouts  12 us (3%)
    all_gather x1, blocking collectives, body(): maps_all = lax.all_gather(x_weight[:, rank:].T, 'dp', axis=0, tiled=False)  120 us
    all_to_all x1, waiting for transfers between devices, body(): lax.all_to_all(scanned_chan.reshape(ndev, tok_dev, chans), 'dp', split_ax...  92.4 us
    pallas_call x1, Pallas kernels, body(): pl.pallas_call(scan_kernel, grid=(total_tok // BLK,), in_specs=[smem, pl....  66.8 us
    all_gather x1, waiting for transfers between devices, body(): proj_all = lax.all_gather(proj, 'dp', axis=0, tiled=True)  44.9 us
    pallas_call x1, Pallas kernels, body(): pl.pallas_call(gate_kernel, grid=(ndev,), in_specs=[smem, pl.BlockSpec((1...  11.8 us
    pallas_call x1, Pallas kernels, body(): pl.pallas_call(proj_kernel, grid=(ndev,), in_specs=[pl.BlockSpec((1, tok_...  11.2 us
    pallas_call x1, Pallas kernels, body(): pl.pallas_call(conv_kernel, grid=(ndev,), in_specs=[smem, pl.BlockSpec((t...  11.1 us
  transfers between devices with their start and end apart: 5, of which 3 were waited for; matrix products, arithmetic and copies ran while one was open for 1% of the time, Pallas kernels for 6%

profile of v3, /device:TPU:13, one launch (start us, length us, event | category | flops | bytes accessed | tf_op | source)
XLA Modules:
  0.0 400.1 jit_solution(13296336387877972334)
XLA Ops:
  6.5 0.0 all-gather.4.cloned.1.call-start
  6.5 1.0 slice.10
  7.5 0.9 copy.13
  8.4 0.0 all-gather.4.cloned.1.call-update
  8.4 0.9 slice.9
  9.3 3.7 collective-permute-start
  13.0 0.7 broadcast_in_dim.9.b_ref
  13.8 0.7 dynamic_slice.7.first_ref
  14.5 0.4 collective-permute-done.halo_ref
  14.9 0.0 copy-start.4
  14.9 0.8 copy-done.4
  15.8 11.1 %conv.1.conv_ref = bf16[16,256,512]{2,1,0:T(8,128)(2,1)S(1)} custom-call(s32[2]{0:T(128)S(1)} %dynamic_slice.7.first_ref, bf16[256,8192]{1,0:T(8,128)(2,1)} %x_ref.1, bf16[8,8192]{1,0:T(8,128)(2,1)S(1)} %collective-permute-done.halo_ref, bf16[4,8192]{1,0:T(4,128)(2,1)S(1)} %copy-done.4, bf16[1,8192]{1,0:T(2,128)(2,1)S(1)} %broadcast_in_dim.9.b_ref), custom_call_target="tpu_custom_call" | custom-call | flops 41943040 | bytes 8388608 | tf_op jit(solution)/shard_map/conv/pallas_call | solution.py:186
  26.9 0.0 copy-start
  26.9 2.0 copy-done
  28.9 7.2 %all-to-all-start = ((bf16[16,256,512]{2,1,0:T(8,128)(2,1)}), bf16[16,256,512]{2,1,0:T(8,128)(2,1)}, u32[]{:S(2)}, u32[]{:S(2)}) async-start(bf16[16,256,512]{2,1,0:T(8,128)(2,1)} %copy-done), calls=%async_computation | async-start | bytes 8388608 | tf_op jit(solution)/shard_map/all_to_all | solution.py:205
  36.1 0.0 all-gather.6.cloned.1.call-start
  36.1 0.8 slice_bitcast_fusion
  36.9 119.6 %all-gather = bf16[512,512]{1,0:T(8,128)(2,1)S(1)} all-gather(bf16[32,512]{1,0:T(8,128)(2,1)S(1)} %slice_bitcast_fusion), channel_id=2, replica_groups=mesh['parts'=2,'dp'=16] {'dp'}, dimensions={0}, use_global_device_ids=true | all-gather | bytes 557056 | tf_op jit(solution)/shard_map/all_gather | solution.py:182
  156.5 0.0 all-gather.4.cloned.1.call-done.rank_ref
  156.5 0.0 copy-start.1
  156.5 2.2 copy-done.1
  158.6 0.0 copy-start.8
  158.6 0.0 copy-start.3
  158.7 0.0 copy-start.5
  158.7 0.0 copy-start.6
  158.7 0.0 copy-start.7
  158.7 11.2 %proj.1 = bf16[256,288]{1,0:T(8,128)(2,1)} custom-call(bf16[16,256,512]{2,1,0:T(8,128)(2,1)S(1)} %copy-done.1, bf16[8192,256]{1,0:T(8,128)(2,1)} %all-gather.4.cloned.1.call-done.rank_ref, bf16[16,32,512]{2,1,0:T(8,128)(2,1)S(1)} %bitcast.6), custom_call_target="tpu_custom_call" | custom-call | flops 1207959552 | bytes 8912896 | tf_op jit(solution)/shard_map/proj/pallas_call | solution.py:207
  169.9 0.0 all-gather.6.cloned.1.call-update
  169.9 0.0 copy-done.8
  169.9 0.0 all-to-all-done
  170.0 44.9 %all-gather.6.cloned.1.call-done.proj_ref = bf16[4096,288]{1,0:T(8,128)(2,1)} async-done(((bf16[256,288]{1,0:T(8,128)(2,1)}), bf16[4096,288]{1,0:T(8,128)(2,1)}) %all-gather.6.cloned.1.call-update) | async-done | bytes 2359312 | tf_op jit(solution)/shard_map/all_gather | solution.py:226
  214.8 0.0 copy-done.3
  214.8 0.0 copy-done.5
  214.8 0.0 copy-done.6
  214.8 0.0 copy-done.7
  214.8 0.0 copy-start.2
  214.8 1.9 copy-done.2
  216.7 66.8 %scan.1 = bf16[4096,512]{1,0:T(8,128)(2,1)} custom-call(s32[32]{0:T(128)S(1)} %copy-done.7, bf16[4096,512]{1,0:T(8,128)(2,1)} %bitcast.conv_ref, bf16[4096,288]{1,0:T(8,128)(2,1)S(1)} %copy-done.2, bf16[256,512]{1,0:T(8,128)(2,1)S(1)} %copy-done.3, bf16[1,512]{1,0:T(2,128)(2,1)S(1)} %broadcast_in_dim.10.dtb_ref, f32[16,512]{1,0:T(8,128)S(1)} %copy-done.5, ...), custom_call_target="tpu_custom_call" | custom-call | tf_op jit(solution)/shard_map/scan/pallas_call | solution.py:229
  283.6 0.0 copy-start.9
  283.6 5.4 %all-to-all-start.1 = ((bf16[16,256,512]{2,1,0:T(8,128)(2,1)}), bf16[16,256,512]{2,1,0:T(8,128)(2,1)}, u32[]{:S(2)}, u32[]{:S(2)}) async-start(bf16[16,256,512]{2,1,0:T(8,128)(2,1)} %bitcast.8), calls=%async_computation.1 | async-start | bytes 8388608 | tf_op jit(solution)/shard_map/all_to_all | solution.py:263
  288.9 0.0 copy-done.9
  288.9 0.1 dynamic_slice.6.live_ref
  289.0 92.4 %all-to-all-done.1.scanned_ref = bf16[16,256,512]{2,1,0:T(8,128)(2,1)} async-done(((bf16[16,256,512]{2,1,0:T(8,128)(2,1)}), bf16[16,256,512]{2,1,0:T(8,128)(2,1)}, u32[]{:S(2)}, u32[]{:S(2)}) %all-to-all-start.1) | async-done | bytes 4194336 | tf_op jit(solution)/shard_map/all_to_all | solution.py:263
  381.4 11.8 %gate.1 = bf16[256,8192]{1,0:T(8,128)(2,1)} custom-call(s32[2]{0:T(128)S(1)} %dynamic_slice.6.live_ref, bf16[16,256,512]{2,1,0:T(8,128)(2,1)} %all-to-all-done.1.scanned_ref, bf16[256,8192]{1,0:T(8,128)(2,1)} %gate_ref.1), custom_call_target="tpu_custom_call" | custom-call | tf_op jit(solution)/shard_map/gate/pallas_call | solution.py:266
  (1 shorter events, 0.0 us)
Async XLA Ops:
  6.5 149.9 %all-gather.4.cloned.1.call-start = ((), (), s32[]{:S(2)}) async-start(), calls=%async_computation.2 | async-start | bytes 4456448 | tf_op jit(solution)/shard_map/all_gather | solution.py:181
  9.3 5.6 %collective-permute-start = (bf16[8,8192]{1,0:T(8,128)(2,1)S(1)}, bf16[8,8192]{1,0:T(8,128)(2,1)S(1)}, u32[]{:S(2)}, u32[]{:S(2)}) collective-permute-start(bf16[8,8192]{1,0:T(8,128)(2,1)S(1)} %slice.9), channel_id=1, source_target_pairs={{0,1},{1,2},{2,3},{3,4},{4,5},{5,6},{6,7},{7,8},{8,9},{9,10},{10,1... | collective-permute-start | bytes 393224 | tf_op jit(solution)/shard_map/ppermute | solution.py:19
  14.9 0.8 copy-start.4
  26.9 2.0 copy-start
  28.9 141.1 %all-to-all-start = ((bf16[16,256,512]{2,1,0:T(8,128)(2,1)}), bf16[16,256,512]{2,1,0:T(8,128)(2,1)}, u32[]{:S(2)}, u32[]{:S(2)}) async-start(bf16[16,256,512]{2,1,0:T(8,128)(2,1)} %copy-done), calls=%async_computation | async-start | bytes 8388608 | tf_op jit(solution)/shard_map/all_to_all | solution.py:205
  36.1 178.7 %all-gather.6.cloned.1.call-start = ((), (), s32[]{:S(2)}) async-start(), calls=%async_computation.3 | async-start | bytes 3342336 | tf_op jit(solution)/shard_map/all_gather | solution.py:226
  156.5 2.2 copy-start.1
  158.6 11.3 %copy-start.8 = (bf16[512]{0:T(512)(128)(2,1)S(1)}, bf16[512]{0:T(512)(128)(2,1)}, u32[]{:S(2)}) copy-start(bf16[512]{0:T(512)(128)(2,1)} %param.18) | copy-start | bytes 3076
  158.6 56.2 %copy-start.3 = (bf16[256,512]{1,0:T(8,128)(2,1)S(1)}, bf16[256,512]{1,0:T(8,128)(2,1)}, u32[]{:S(2)}) copy-start(bf16[256,512]{1,0:T(8,128)(2,1)} %dtw_ref.1) | copy-start | bytes 786436
  158.7 56.2 %copy-start.5 = (f32[16,512]{1,0:T(8,128)S(1)}, f32[16,512]{1,0:T(8,128)}, u32[]{:S(2)}) copy-start(f32[16,512]{1,0:T(8,128)} %alog_ref.1) | copy-start | bytes 98308
  158.7 56.2 %copy-start.6 = (f32[512]{0:T(512)S(1)}, f32[512]{0:T(512)}, u32[]{:S(2)}) copy-start(f32[512]{0:T(512)} %param.20) | copy-start | bytes 6148
  158.7 56.2 %copy-start.7 = (s32[32]{0:T(128)S(1)}, s32[32]{0:T(128)}, u32[]{:S(2)}) copy-start(s32[32]{0:T(128)} %first_ref.1) | copy-start | bytes 388
  214.8 1.9 copy-start.2
  283.6 5.4 %copy-start.9 = (s32[32]{0:T(128)S(1)}, s32[32]{0:T(128)}, u32[]{:S(2)}) copy-start(s32[32]{0:T(128)} %param.22) | copy-start | bytes 388
  283.6 97.9 %all-to-all-start.1 = ((bf16[16,256,512]{2,1,0:T(8,128)(2,1)}), bf16[16,256,512]{2,1,0:T(8,128)(2,1)}, u32[]{:S(2)}, u32[]{:S(2)}) async-start(bf16[16,256,512]{2,1,0:T(8,128)(2,1)} %bitcast.8), calls=%async_computation.1 | async-start | bytes 8388608 | tf_op jit(solution)/shard_map/all_to_all | solution.py:263
Sparse Core Ops, SparseCore 0:
  9.5 87.4 all-gather.3
  170.0 44.7 all-gather.5
